TPU v7x, 32 devices: a whole 2x2x4 slice. The times are simulated.
32 devices in a mesh: depth: 8 (over y, x, core), rows: 4 (over z).
Axes of the slice: x: 2, y: 2, z: 4, core: 2. Of those that a mesh axis runs over, the one named last changes fastest.
Arguments:
- initial: float32 [16, 256, 128], P('rows'), may hold values from -6 to 6
- forward_guess: float32 [16, 16, 256, 128], P('depth', 'rows'), may hold values from -6 to 6
- adjoint_guess: float32 [16, 16, 256, 128], P('depth', 'rows'), may hold values from -6 to 6
- cotangent: float32 [16, 256, 128], P('rows'), may hold values from -6 to 6
- kernel: bfloat16 [3, 3, 128, 128], replicated, may hold values from -0.125 to 0.125
- conv_bias: float32 [128], replicated, may hold values from -1.5 to 1.5
Outputs:
- states: float32 [16, 16, 256, 128], P('depth', 'rows')
- adjoints: float32 [16, 16, 256, 128], P('depth', 'rows')
- grad_kernel: float32 [3, 3, 128, 128], replicated
- grad_bias: float32 [128], replicated
All inputs are finite; a program needn't handle non-finite values.
Results may differ from a plain program's by a relative error of at most 0.0025.
The roundings to bfloat16 on the way count: a program that leaves them out, or rounds other values in their place, can miss the bound.
Values may be sent and summed in bfloat16 or wider, within the bound.
A program may use at most 64 MiB of HBM per device.

v0:
```python
import jax
import jax.numpy as jnp
from jax import lax
from jax.sharding import PartitionSpec as P

STEP_SIZE = 0.2


def padded_2(shard, sides, width):
    for axis, dim in sides:
        devices, length = (lax.axis_size(axis), shard.shape[dim])
        up = [(i, (i + 1) % devices) for i in range(devices - 1)]
        down = [(j, i) for i, j in up]
        last = lax.slice_in_dim(shard, length - width, length, axis=dim)
        leading = lax.slice_in_dim(shard, 0, width, axis=dim)
        before = lax.ppermute(last, axis, up)
        after = lax.ppermute(leading, axis, down)
        shard = jnp.concatenate([before, shard, after], axis=dim)
    return shard


def passed_along(value, axis, steps):
    count = lax.axis_size(axis)
    leading, last = (max(0, -steps), min(count, count - steps))
    return lax.ppermute(value, axis, [(source, source + steps) for source in range(leading, last)])


def restrict(signal):
    row_count, col_count, channels = signal.shape
    return signal.reshape(row_count // 2, 2, col_count // 2, 2, channels).mean(axis=(1, 3))


def prolong(signal):
    return jnp.repeat(jnp.repeat(signal, 2, axis=0), 2, axis=1)


def taps_product(padded, kernel, row_count, col_count):
    summed = jnp.zeros((row_count * col_count, kernel.shape[3]), jnp.float32)
    for row_tap in range(3):
        for col_tap in range(3):
            window = padded[row_tap : row_tap + row_count, col_tap : col_tap + col_count].reshape(
                row_count * col_count, -1
            )
            summed = summed + jnp.dot(
                window, kernel[row_tap, col_tap], preferred_element_type=jnp.float32
            )
    return summed.reshape(row_count, col_count, -1)


def surround(signal, on_coarse):
    if on_coarse:
        padded = padded_2(signal, (("rows", 0),), 1)
    else:
        padded = padded_2(signal, (("rows", 0),), 1)
    return jnp.pad(padded, ((0, 0), (1, 1), (0, 0)))


def advance(current, kernel, conv_bias, on_coarse):
    factor = 2.0 * STEP_SIZE if on_coarse else STEP_SIZE
    squashed = jnp.tanh(current).astype(jnp.bfloat16)
    padded = surround(squashed, on_coarse)
    return current + factor * (
        taps_product(padded, kernel, current.shape[0], current.shape[1]) + conv_bias
    )


def retreat(current, adjoint, kernel_flip, on_coarse):
    factor = 2.0 * STEP_SIZE if on_coarse else STEP_SIZE
    derivative = 1.0 - jnp.tanh(current) ** 2
    padded = surround(adjoint.astype(jnp.bfloat16), on_coarse)
    return adjoint + factor * derivative * taps_product(
        padded, kernel_flip, adjoint.shape[0], adjoint.shape[1]
    )


def kernel_terms(padded, cotan, row_count, col_count):
    flat = cotan.reshape(row_count * col_count, -1)
    tap_rows = []
    for row_tap in range(3):
        tap_cols = []
        for col_tap in range(3):
            window = padded[row_tap : row_tap + row_count, col_tap : col_tap + col_count].reshape(
                row_count * col_count, -1
            )
            tap_cols.append(
                lax.dot_general(
                    window, flat, (((0,), (0,)), ((), ())), preferred_element_type=jnp.float32
                )
            )
        tap_rows.append(jnp.stack(tap_cols))
    return jnp.stack(tap_rows)


def shards(initial, forward_guess, adjoint_guess, cotangent, kernel, conv_bias):
    block_count = lax.axis_size("depth")
    depth_pos = lax.axis_index("depth")
    at_first = depth_pos == 0
    at_last = depth_pos == block_count - 1
    row_count, col_count = (initial.shape[0], initial.shape[1])
    kernel_flip = jnp.transpose(jnp.flip(kernel, (0, 1)), (0, 1, 3, 2))
    coarse_start = restrict(initial)
    guess_point = forward_guess[1]
    previous = passed_along(guess_point, "depth", 1)
    previous = jnp.where(at_first, initial, previous)
    relaxed_odd = advance(previous, kernel, conv_bias, False)
    rhs_local = restrict(advance(relaxed_odd, kernel, conv_bias, False)) - advance(
        restrict(previous), kernel, conv_bias, True
    )
    panels = lax.all_gather(rhs_local[None], "depth", axis=0, tiled=True)

    def solve_coarse(solution, panel):
        solution = advance(solution, kernel, conv_bias, True) + panel
        return (solution, solution)

    last_coarse, solutions = lax.scan(solve_coarse, coarse_start, panels)
    stored = lax.dynamic_index_in_dim(solutions, depth_pos, 0, keepdims=False)
    corrected = guess_point + prolong(stored - restrict(guess_point))
    prev_fixed, prev_coarse = passed_along((corrected, stored), "depth", 1)
    prev_fixed = jnp.where(at_first, initial, prev_fixed)
    state_odd = advance(prev_fixed, kernel, conv_bias, False)
    guess_even = adjoint_guess[0]
    ahead = passed_along(guess_even, "depth", -1)
    ahead = jnp.where(at_last, cotangent, ahead)
    relaxed_adj = retreat(state_odd, ahead, kernel_flip, False)
    residual = retreat(prev_fixed, relaxed_adj, kernel_flip, False) - guess_even
    coarse_res = restrict(residual)
    res_panels = lax.all_gather(coarse_res[None], "depth", axis=0, tiled=True)

    def backward_solve(step_no, state_pair):
        correction, kept_error = state_pair
        coarse_no = block_count - 1 - step_no
        earlier = lax.dynamic_index_in_dim(
            solutions, jnp.maximum(coarse_no - 1, 0), 0, keepdims=False
        )
        linear_here = jnp.where(coarse_no == 0, coarse_start, earlier)
        correction = retreat(linear_here, correction, kernel_flip, True) + lax.dynamic_index_in_dim(
            res_panels, coarse_no, 0, keepdims=False
        )
        kept_error = jnp.where(coarse_no == depth_pos, correction, kept_error)
        return (correction, kept_error)

    final_error, error_own = lax.fori_loop(
        0, block_count, backward_solve, (jnp.zeros_like(coarse_start), jnp.zeros_like(coarse_start))
    )
    corrected_adj = guess_even + prolong(error_own)
    ahead_fixed = passed_along(corrected_adj, "depth", -1)
    ahead_fixed = jnp.where(at_last, cotangent, ahead_fixed)
    adjoint_odd = retreat(state_odd, ahead_fixed, kernel_flip, False)
    squashed_even = surround(jnp.tanh(prev_fixed).astype(jnp.bfloat16), False)
    squashed_odd = surround(jnp.tanh(state_odd).astype(jnp.bfloat16), False)
    local_grad = kernel_terms(squashed_even, adjoint_odd.astype(jnp.bfloat16), row_count, col_count)
    local_grad = local_grad + kernel_terms(
        squashed_odd, ahead_fixed.astype(jnp.bfloat16), row_count, col_count
    )
    local_bias = jnp.sum(adjoint_odd, axis=(0, 1)) + jnp.sum(ahead_fixed, axis=(0, 1))
    grad_sum, bias_sum = lax.psum((local_grad, local_bias), ("depth", "rows"))
    factor = STEP_SIZE / (row_count * lax.axis_size("rows") * col_count)
    states_out = jnp.stack([state_odd, corrected])
    adjoints_out = jnp.stack([corrected_adj, adjoint_odd])
    return (states_out, adjoints_out, grad_sum * factor, bias_sum * factor)


def solution(mesh):
    placed = (
        P("rows", None, None),
        P("depth", "rows", None, None),
        P("depth", "rows", None, None),
        P("rows", None, None),
        P(),
        P(),
    )
    return jax.shard_map(
        shards,
        mesh=mesh,
        in_specs=placed,
        out_specs=(P("depth", "rows", None, None), P("depth", "rows", None, None), P(), P()),
        check_vma=False,
    )
```

profile of v0, /device:TPU:0, one launch (start us, length us, event | category | flops | bytes accessed | tf_op | source)
XLA Modules:
  0.0 630.1 jit_solution(17837151883567481940)
XLA Ops:
  11.2 3.8 collective-permute-start.4
  24.4 5.6 collective-permute-start.9
  31.5 4.5 collective-permute-start.15
  37.3 4.5 collective-permute-start.5
  45.8 2.7 collective-permute-done.6
  75.9 2.9 collective-permute-start.7
  81.7 3.4 collective-permute-done.8
  107.3 2.0 copy.161
  109.3 2.2 multiply_add_fusion.3
  111.5 2.1 copy.162
  133.8 9.2 %all-gather.4.cloned.1.call-done = f32[8,2,128,128]{3,2,1,0:T(8,128)} async-done(((f32[1,2,128,128]{3,2,1,0:T(8,128)}), f32[8,2,128,128]{3,2,1,0:T(8,128)}) %all-gather.4.cloned.1.call-update) | async-done | bytes 1048592 | tf_op jit(solution)/shard_map/all_gather | solution.py:109
  143.0 87.3 %while.34 = (s32[]{:T(128)}, f32[2,128,128]{2,1,0:T(8,128)S(1)}, f32[8,2,128,128]{3,2,1,0:T(8,128)}, bf16[3,3,128,128]{3,2,1,0:T(8,128)(2,1)S(1)}, f32[128]{0:T(128)S(1)}, /*index=5*/f32[8,2,128,128]{3,2,1,0:T(8,128)}, s32[]{:T(128)}) while((s32[]{:T(128)}, f32[2,128,128]{2,1,0:T(8,128)S(1)}, f32[8,2,128,128]{3,2,1,0:T(8,128)}, ...), condition=%wide.region_4.5_spmd, body=%wide.region_3.4_spmd.sunk | while | flops 76787712 | bytes 5671593 | solution.py:115
  144.5 4.5 collective-permute-start.1
  155.1 4.9 collective-permute-start.1
  166.0 4.9 collective-permute-start.1
  176.9 4.9 collective-permute-start.1
  187.9 4.9 collective-permute-start.1
  198.8 4.9 collective-permute-start.1
  209.7 4.9 collective-permute-start.1
  220.7 4.9 collective-permute-start.1
  232.5 2.2 collective-permute-start.11
  240.9 4.2 collective-permute-start.12
  248.5 2.8 collective-permute-done.13
  273.1 2.1 tanh_convert_fusion.3
  276.2 3.9 collective-permute-start.17
  282.5 3.8 collective-permute-done.18
  308.3 2.0 copy.200
  310.3 2.3 add_subtract_fusion
  312.6 2.1 copy.201
  316.9 27.7 %all-gather.6.cloned.1.call-done = f32[16,128,128]{2,1,0:T(8,128)} async-done(((f32[2,128,128]{2,1,0:T(8,128)}), f32[16,128,128]{2,1,0:T(8,128)}) %all-gather.6.cloned.1.call-update) | async-done | bytes 1048592 | tf_op jit(solution)/shard_map/all_gather | solution.py:127
  344.5 88.8 %while.35 = (s32[]{:T(128)}, f32[2,128,128]{2,1,0:T(8,128)S(1)}, f32[2,128,128]{2,1,0:T(8,128)}, f32[8,2,128,128]{3,2,1,0:T(8,128)}, f32[2,128,128]{2,1,0:T(8,12...) while((s32[]{:T(128)}, f32[2,128,128]{2,1,0:T(8,128)S(1)}, ...), condition=%wide.region_8.9_spmd.clone, body=%wide.region_7.8_spmd.clone.sunk | while | flops 76984328 | bytes 7113074 | solution.py:142
  345.9 4.5 collective-permute-start.3
  356.7 4.9 collective-permute-start.3
  367.8 4.9 collective-permute-start.3
  379.0 4.9 collective-permute-start.3
  390.1 4.9 collective-permute-start.3
  401.2 4.9 collective-permute-start.3
  412.4 4.9 collective-permute-start.3
  423.5 4.9 collective-permute-start.3
  435.2 2.0 copy.203
  440.4 2.0 copy.177
  443.7 4.2 collective-permute-start.22
  450.3 2.5 copy.233
  455.8 2.0 copy.202
  464.3 3.9 collective-permute-start.20
  471.7 2.7 collective-permute-done.21
  495.7 40.6 %psum.15 = f32[128]{0:T(128)S(1)} all-reduce(f32[128]{0:T(128)S(1)} %add.608), channel_id=1, replica_groups=mesh['depth'=8,'rows'=4] {'depth','rows'}, use_global_device_ids=true, to_apply=%region_12.13 | all-reduce | flops 128 | bytes 1024 | tf_op jit(solution)/shard_map/psum | solution.py:156
  536.8 84.8 %all-reduce.12.cloned.1.call-done = f32[3,3,128,128]{3,2,1,0:T(8,128)} async-done(((f32[3,3,128,128]{3,2,1,0:T(8,128)}), f32[3,3,128,128]{3,2,1,0:T(8,128)}) %all-reduce.12.cloned.1.call-update) | async-done | bytes 589840 | tf_op jit(solution)/shard_map/psum | solution.py:156
  (742 shorter events, 294.7 us)
Async XLA Ops:
  7.2 135.8 %all-gather.4.cloned.1.call-start = ((), (), s32[]{:S(2)}) async-start(), calls=%async_computation | async-start | bytes 1179648 | tf_op jit(solution)/shard_map/all_gather | solution.py:109
  8.4 10.1 %collective-permute-start.14 = (f32[4,256,128]{1,2,0:T(8,128)S(1)}, f32[4,256,128]{1,2,0:T(8,128)S(1)}, u32[]{:S(2)}, u32[]{:S(2)}) collective-permute-start(f32[4,256,128]{1,2,0:T(8,128)S(1)} %bitcast.609), channel_id=1, source_target_pairs={{4,0},{8,4},{12,8},{16,12},{20,16},{24,20},{28,24},{5,1},{9,5},{13... | collective-permute-start | bytes 1572872 | tf_op jit(solution)/shard_map/ppermute | solution.py:25
  11.2 8.3 %collective-permute-start.4 = (f32[4,256,128]{1,2,0:T(8,128)S(1)}, f32[4,256,128]{1,2,0:T(8,128)}, u32[]{:S(2)}, u32[]{:S(2)}) collective-permute-start(f32[4,256,128]{1,2,0:T(8,128)S(1)} %bitcast.627), channel_id=1, source_target_pairs={{0,4},{4,8},{8,12},{12,16},{16,20},{20,24},{24,28},{1,5},{5,9},{9,... | collective-permute-start | bytes 1572872 | tf_op jit(solution)/shard_map/ppermute | solution.py:25
  23.1 18.8 %collective-permute-start.10 = (bf16[1,128,128]{2,1,0:T(8,128)(2,1)S(1)}, bf16[1,128,128]{2,1,0:T(8,128)(2,1)S(1)}, u32[]{:S(2)}, u32[]{:S(2)}) collective-permute-start(bf16[1,128,128]{2,1,0:T(8,128)(2,1)S(1)} %get-tuple-element.516), channel_id=1, source_target_pairs={{1,0},{2,1},{3,2},{5,4},{6,5},{7,6},{9,8},{10,9},{11,10},{13,12},{... | collective-permute-start | bytes 98312 | tf_op jit(solution)/shard_map/ppermute | solution.py:17
  24.4 18.8 %collective-permute-start.9 = (bf16[1,128,128]{2,1,0:T(8,128)(2,1)S(1)}, bf16[1,128,128]{2,1,0:T(8,128)(2,1)S(1)}, u32[]{:S(2)}, u32[]{:S(2)}) collective-permute-start(bf16[1,128,128]{2,1,0:T(8,128)(2,1)S(1)} %get-tuple-element.515), channel_id=1, source_target_pairs={{0,1},{1,2},{2,3},{4,5},{5,6},{6,7},{8,9},{9,10},{10,11},{12,13},{... | collective-permute-start | bytes 98312 | tf_op jit(solution)/shard_map/ppermute | solution.py:16
  31.5 87.5 %collective-permute-start.15 = (bf16[1,256,128]{1,2,0:T(8,128)(2,1)}, bf16[1,256,128]{1,2,0:T(8,128)(2,1)}, u32[]{:S(2)}, u32[]{:S(2)}) collective-permute-start(bf16[1,256,128]{1,2,0:T(8,128)(2,1)} %get-tuple-element.493), channel_id=1, source_target_pairs={{0,1},{1,2},{2,3},{4,5},{5,6},{6,7},{8,9},{9,10},{10,11},{12,13},{... | collective-permute-start | bytes 196616 | tf_op jit(solution)/shard_map/ppermute | solution.py:16
  36.0 82.9 %collective-permute-start.16 = (bf16[1,256,128]{1,2,0:T(8,128)(2,1)}, bf16[1,256,128]{1,2,0:T(8,128)(2,1)}, u32[]{:S(2)}, u32[]{:S(2)}) collective-permute-start(bf16[1,256,128]{1,2,0:T(8,128)(2,1)} %get-tuple-element.494), channel_id=1, source_target_pairs={{1,0},{2,1},{3,2},{5,4},{6,5},{7,6},{9,8},{10,9},{11,10},{13,12},{... | collective-permute-start | bytes 196616 | tf_op jit(solution)/shard_map/ppermute | solution.py:17
  37.3 8.5 %collective-permute-start.5 = (bf16[1,256,128]{1,2,0:T(8,128)(2,1)}, bf16[1,256,128]{1,2,0:T(8,128)(2,1)S(1)}, u32[]{:S(2)}, u32[]{:S(2)}) collective-permute-start(bf16[1,256,128]{1,2,0:T(8,128)(2,1)} %get-tuple-element.505), channel_id=1, source_target_pairs={{0,1},{1,2},{2,3},{4,5},{5,6},{6,7},{8,9},{9,10},{10,11},{12,13},{... | collective-permute-start | bytes 196616 | tf_op jit(solution)/shard_map/ppermute | solution.py:16
  41.8 6.7 %collective-permute-start.6 = (bf16[1,256,128]{1,2,0:T(8,128)(2,1)}, bf16[1,256,128]{1,2,0:T(8,128)(2,1)S(1)}, u32[]{:S(2)}, u32[]{:S(2)}) collective-permute-start(bf16[1,256,128]{1,2,0:T(8,128)(2,1)} %get-tuple-element.506), channel_id=1, source_target_pairs={{1,0},{2,1},{3,2},{5,4},{6,5},{7,6},{9,8},{10,9},{11,10},{13,12},{... | collective-permute-start | bytes 196616 | tf_op jit(solution)/shard_map/ppermute | solution.py:17
  78.8 6.4 %collective-permute-start.8 = (bf16[1,256,128]{1,2,0:T(8,128)(2,1)}, bf16[1,256,128]{1,2,0:T(8,128)(2,1)S(1)}, u32[]{:S(2)}, u32[]{:S(2)}) collective-permute-start(bf16[1,256,128]{1,2,0:T(8,128)(2,1)} %get-tuple-element.502), channel_id=1, source_target_pairs={{1,0},{2,1},{3,2},{5,4},{6,5},{7,6},{9,8},{10,9},{11,10},{13,12},{... | collective-permute-start | bytes 196616 | tf_op jit(solution)/shard_map/ppermute | solution.py:17
  115.8 228.8 %all-gather.6.cloned.1.call-start = ((), (), s32[]{:S(2)}) async-start(), calls=%async_computation.2 | async-start | bytes 1179648 | tf_op jit(solution)/shard_map/all_gather | solution.py:127
  153.8 6.2 collective-permute-start
  155.1 6.4 %collective-permute-start.1 = (bf16[1,128,128]{2,1,0:T(8,128)(2,1)S(1)}, bf16[1,128,128]{2,1,0:T(8,128)(2,1)S(1)}, u32[]{:S(2)}, u32[]{:S(2)}) collective-permute-start(bf16[1,128,128]{2,1,0:T(8,128)(2,1)S(1)} %get-tuple-element.624), channel_id=1, source_target_pairs={{0,1},{1,2},{2,3},{4,5},{5,6},{6,7},{8,9},{9,10},{10,11},{12,13},{... | collective-permute-start | bytes 98312 | tf_op jit(solution)/shard_map/while/body/eval_jaxpr/ppermute | solution.py:16
  164.7 6.2 collective-permute-start
  166.0 6.4 %collective-permute-start.1 = (bf16[1,128,128]{2,1,0:T(8,128)(2,1)S(1)}, bf16[1,128,128]{2,1,0:T(8,128)(2,1)S(1)}, u32[]{:S(2)}, u32[]{:S(2)}) collective-permute-start(bf16[1,128,128]{2,1,0:T(8,128)(2,1)S(1)} %get-tuple-element.624), channel_id=1, source_target_pairs={{0,1},{1,2},{2,3},{4,5},{5,6},{6,7},{8,9},{9,10},{10,11},{12,13},{... | collective-permute-start | bytes 98312 | tf_op jit(solution)/shard_map/while/body/eval_jaxpr/ppermute | solution.py:16
  175.7 6.2 collective-permute-start
  176.9 6.4 %collective-permute-start.1 = (bf16[1,128,128]{2,1,0:T(8,128)(2,1)S(1)}, bf16[1,128,128]{2,1,0:T(8,128)(2,1)S(1)}, u32[]{:S(2)}, u32[]{:S(2)}) collective-permute-start(bf16[1,128,128]{2,1,0:T(8,128)(2,1)S(1)} %get-tuple-element.624), channel_id=1, source_target_pairs={{0,1},{1,2},{2,3},{4,5},{5,6},{6,7},{8,9},{9,10},{10,11},{12,13},{... | collective-permute-start | bytes 98312 | tf_op jit(solution)/shard_map/while/body/eval_jaxpr/ppermute | solution.py:16
  186.6 6.2 collective-permute-start
  187.9 6.4 %collective-permute-start.1 = (bf16[1,128,128]{2,1,0:T(8,128)(2,1)S(1)}, bf16[1,128,128]{2,1,0:T(8,128)(2,1)S(1)}, u32[]{:S(2)}, u32[]{:S(2)}) collective-permute-start(bf16[1,128,128]{2,1,0:T(8,128)(2,1)S(1)} %get-tuple-element.624), channel_id=1, source_target_pairs={{0,1},{1,2},{2,3},{4,5},{5,6},{6,7},{8,9},{9,10},{10,11},{12,13},{... | collective-permute-start | bytes 98312 | tf_op jit(solution)/shard_map/while/body/eval_jaxpr/ppermute | solution.py:16
  197.5 6.2 collective-permute-start
  198.8 6.4 %collective-permute-start.1 = (bf16[1,128,128]{2,1,0:T(8,128)(2,1)S(1)}, bf16[1,128,128]{2,1,0:T(8,128)(2,1)S(1)}, u32[]{:S(2)}, u32[]{:S(2)}) collective-permute-start(bf16[1,128,128]{2,1,0:T(8,128)(2,1)S(1)} %get-tuple-element.624), channel_id=1, source_target_pairs={{0,1},{1,2},{2,3},{4,5},{5,6},{6,7},{8,9},{9,10},{10,11},{12,13},{... | collective-permute-start | bytes 98312 | tf_op jit(solution)/shard_map/while/body/eval_jaxpr/ppermute | solution.py:16
  208.4 6.2 collective-permute-start
  209.7 6.4 %collective-permute-start.1 = (bf16[1,128,128]{2,1,0:T(8,128)(2,1)S(1)}, bf16[1,128,128]{2,1,0:T(8,128)(2,1)S(1)}, u32[]{:S(2)}, u32[]{:S(2)}) collective-permute-start(bf16[1,128,128]{2,1,0:T(8,128)(2,1)S(1)} %get-tuple-element.624), channel_id=1, source_target_pairs={{0,1},{1,2},{2,3},{4,5},{5,6},{6,7},{8,9},{9,10},{10,11},{12,13},{... | collective-permute-start | bytes 98312 | tf_op jit(solution)/shard_map/while/body/eval_jaxpr/ppermute | solution.py:16
  219.4 6.2 collective-permute-start
  220.7 6.4 %collective-permute-start.1 = (bf16[1,128,128]{2,1,0:T(8,128)(2,1)S(1)}, bf16[1,128,128]{2,1,0:T(8,128)(2,1)S(1)}, u32[]{:S(2)}, u32[]{:S(2)}) collective-permute-start(bf16[1,128,128]{2,1,0:T(8,128)(2,1)S(1)} %get-tuple-element.624), channel_id=1, source_target_pairs={{0,1},{1,2},{2,3},{4,5},{5,6},{6,7},{8,9},{9,10},{10,11},{12,13},{... | collective-permute-start | bytes 98312 | tf_op jit(solution)/shard_map/while/body/eval_jaxpr/ppermute | solution.py:16
  232.5 7.4 %collective-permute-start.11 = (f32[4,256,128]{1,2,0:T(8,128)}, f32[4,256,128]{1,2,0:T(8,128)}, u32[]{:S(2)}, u32[]{:S(2)}) collective-permute-start(f32[4,256,128]{1,2,0:T(8,128)} %bitcast_add_fusion.4), channel_id=1, source_target_pairs={{0,4},{4,8},{8,12},{12,16},{16,20},{20,24},{24,28},{1,5},{5,9},{9,... | collective-permute-start | bytes 1572872 | tf_op jit(solution)/shard_map/ppermute | solution.py:25
  240.9 7.6 %collective-permute-start.12 = (bf16[1,256,128]{1,2,0:T(8,128)(2,1)S(1)}, bf16[1,256,128]{1,2,0:T(8,128)(2,1)S(1)}, u32[]{:S(2)}, u32[]{:S(2)}) collective-permute-start(bf16[1,256,128]{1,2,0:T(8,128)(2,1)S(1)} %get-tuple-element.497), channel_id=1, source_target_pairs={{0,1},{1,2},{2,3},{4,5},{5,6},{6,7},{8,9},{9,10},{10,11},{12,13},{... | collective-permute-start | bytes 196616 | tf_op jit(solution)/shard_map/ppermute | solution.py:16
  276.2 6.3 %collective-permute-start.17 = (bf16[1,256,128]{1,2,0:T(8,128)(2,1)S(1)}, bf16[1,256,128]{1,2,0:T(8,128)(2,1)S(1)}, u32[]{:S(2)}, u32[]{:S(2)}) collective-permute-start(bf16[1,256,128]{1,2,0:T(8,128)(2,1)S(1)} %get-tuple-element.489), channel_id=1, source_target_pairs={{0,1},{1,2},{2,3},{4,5},{5,6},{6,7},{8,9},{9,10},{10,11},{12,13},{... | collective-permute-start | bytes 196616 | tf_op jit(solution)/shard_map/ppermute | solution.py:16
  316.8 304.8 %all-reduce.12.cloned.1.call-start = ((), (), s32[]{:S(2)}) async-start(), calls=%async_computation.1 | async-start | bytes 1179648 | tf_op jit(solution)/shard_map/psum | solution.py:156
  355.4 6.2 collective-permute-start.2
  356.7 6.4 %collective-permute-start.3 = (bf16[1,128,128]{2,1,0:T(8,128)(2,1)S(1)}, bf16[1,128,128]{2,1,0:T(8,128)(2,1)S(1)}, u32[]{:S(2)}, u32[]{:S(2)}) collective-permute-start(bf16[1,128,128]{2,1,0:T(8,128)(2,1)S(1)} %get-tuple-element.644), channel_id=1, source_target_pairs={{0,1},{1,2},{2,3},{4,5},{5,6},{6,7},{8,9},{9,10},{10,11},{12,13},{... | collective-permute-start | bytes 98312 | tf_op jit(solution)/shard_map/while/body/eval_jaxpr/ppermute | solution.py:16
  366.5 6.2 collective-permute-start.2
  367.8 6.4 %collective-permute-start.3 = (bf16[1,128,128]{2,1,0:T(8,128)(2,1)S(1)}, bf16[1,128,128]{2,1,0:T(8,128)(2,1)S(1)}, u32[]{:S(2)}, u32[]{:S(2)}) collective-permute-start(bf16[1,128,128]{2,1,0:T(8,128)(2,1)S(1)} %get-tuple-element.644), channel_id=1, source_target_pairs={{0,1},{1,2},{2,3},{4,5},{5,6},{6,7},{8,9},{9,10},{10,11},{12,13},{... | collective-permute-start | bytes 98312 | tf_op jit(solution)/shard_map/while/body/eval_jaxpr/ppermute | solution.py:16
  377.7 6.2 collective-permute-start.2
  379.0 6.4 %collective-permute-start.3 = (bf16[1,128,128]{2,1,0:T(8,128)(2,1)S(1)}, bf16[1,128,128]{2,1,0:T(8,128)(2,1)S(1)}, u32[]{:S(2)}, u32[]{:S(2)}) collective-permute-start(bf16[1,128,128]{2,1,0:T(8,128)(2,1)S(1)} %get-tuple-element.644), channel_id=1, source_target_pairs={{0,1},{1,2},{2,3},{4,5},{5,6},{6,7},{8,9},{9,10},{10,11},{12,13},{... | collective-permute-start | bytes 98312 | tf_op jit(solution)/shard_map/while/body/eval_jaxpr/ppermute | solution.py:16
  388.8 6.2 collective-permute-start.2
  390.1 6.4 %collective-permute-start.3 = (bf16[1,128,128]{2,1,0:T(8,128)(2,1)S(1)}, bf16[1,128,128]{2,1,0:T(8,128)(2,1)S(1)}, u32[]{:S(2)}, u32[]{:S(2)}) collective-permute-start(bf16[1,128,128]{2,1,0:T(8,128)(2,1)S(1)} %get-tuple-element.644), channel_id=1, source_target_pairs={{0,1},{1,2},{2,3},{4,5},{5,6},{6,7},{8,9},{9,10},{10,11},{12,13},{... | collective-permute-start | bytes 98312 | tf_op jit(solution)/shard_map/while/body/eval_jaxpr/ppermute | solution.py:16
  399.9 6.2 collective-permute-start.2
  401.2 6.4 %collective-permute-start.3 = (bf16[1,128,128]{2,1,0:T(8,128)(2,1)S(1)}, bf16[1,128,128]{2,1,0:T(8,128)(2,1)S(1)}, u32[]{:S(2)}, u32[]{:S(2)}) collective-permute-start(bf16[1,128,128]{2,1,0:T(8,128)(2,1)S(1)} %get-tuple-element.644), channel_id=1, source_target_pairs={{0,1},{1,2},{2,3},{4,5},{5,6},{6,7},{8,9},{9,10},{10,11},{12,13},{... | collective-permute-start | bytes 98312 | tf_op jit(solution)/shard_map/while/body/eval_jaxpr/ppermute | solution.py:16
  411.1 6.2 collective-permute-start.2
  412.4 6.4 %collective-permute-start.3 = (bf16[1,128,128]{2,1,0:T(8,128)(2,1)S(1)}, bf16[1,128,128]{2,1,0:T(8,128)(2,1)S(1)}, u32[]{:S(2)}, u32[]{:S(2)}) collective-permute-start(bf16[1,128,128]{2,1,0:T(8,128)(2,1)S(1)} %get-tuple-element.644), channel_id=1, source_target_pairs={{0,1},{1,2},{2,3},{4,5},{5,6},{6,7},{8,9},{9,10},{10,11},{12,13},{... | collective-permute-start | bytes 98312 | tf_op jit(solution)/shard_map/while/body/eval_jaxpr/ppermute | solution.py:16
  422.2 6.2 collective-permute-start.2
  423.5 6.4 %collective-permute-start.3 = (bf16[1,128,128]{2,1,0:T(8,128)(2,1)S(1)}, bf16[1,128,128]{2,1,0:T(8,128)(2,1)S(1)}, u32[]{:S(2)}, u32[]{:S(2)}) collective-permute-start(bf16[1,128,128]{2,1,0:T(8,128)(2,1)S(1)} %get-tuple-element.644), channel_id=1, source_target_pairs={{0,1},{1,2},{2,3},{4,5},{5,6},{6,7},{8,9},{9,10},{10,11},{12,13},{... | collective-permute-start | bytes 98312 | tf_op jit(solution)/shard_map/while/body/eval_jaxpr/ppermute | solution.py:16
  439.2 20.6 %collective-permute-start.19 = (f32[4,256,128]{1,2,0:T(8,128)}, f32[4,256,128]{1,2,0:T(8,128)}, u32[]{:S(2)}, u32[]{:S(2)}) collective-permute-start(f32[4,256,128]{1,2,0:T(8,128)} %bitcast_add_fusion.3), channel_id=1, source_target_pairs={{4,0},{8,4},{12,8},{16,12},{20,16},{24,20},{28,24},{5,1},{9,5},{13... | collective-permute-start | bytes 1572872 | tf_op jit(solution)/shard_map/ppermute | solution.py:25
  443.7 9.1 %collective-permute-start.22 = (bf16[1,256,128]{1,2,0:T(8,128)(2,1)S(1)}, bf16[1,256,128]{1,2,0:T(8,128)(2,1)S(1)}, u32[]{:S(2)}, u32[]{:S(2)}) collective-permute-start(bf16[1,256,128]{1,2,0:T(8,128)(2,1)S(1)} %get-tuple-element.481), channel_id=1, source_target_pairs={{0,1},{1,2},{2,3},{4,5},{5,6},{6,7},{8,9},{9,10},{10,11},{12,13},{... | collective-permute-start | bytes 196616 | tf_op jit(solution)/shard_map/ppermute | solution.py:16
  447.9 6.7 %collective-permute-start.23 = (bf16[1,256,128]{1,2,0:T(8,128)(2,1)S(1)}, bf16[1,256,128]{1,2,0:T(8,128)(2,1)S(1)}, u32[]{:S(2)}, u32[]{:S(2)}) collective-permute-start(bf16[1,256,128]{1,2,0:T(8,128)(2,1)S(1)} %get-tuple-element.482), channel_id=1, source_target_pairs={{1,0},{2,1},{3,2},{5,4},{6,5},{7,6},{9,8},{10,9},{11,10},{13,12},{... | collective-permute-start | bytes 196616 | tf_op jit(solution)/shard_map/ppermute | solution.py:17
  464.3 7.4 %collective-permute-start.20 = (bf16[1,256,128]{1,2,0:T(8,128)(2,1)S(1)}, bf16[1,256,128]{1,2,0:T(8,128)(2,1)S(1)}, u32[]{:S(2)}, u32[]{:S(2)}) collective-permute-start(bf16[1,256,128]{1,2,0:T(8,128)(2,1)S(1)} %copy-done.81), channel_id=1, source_target_pairs={{0,1},{1,2},{2,3},{4,5},{5,6},{6,7},{8,9},{9,10},{10,11},{12,13},{... | collective-permute-start | bytes 196616 | tf_op jit(solution)/shard_map/ppermute | solution.py:16
  468.2 6.2 collective-permute-start.21
  (109 other events, 508.5 us)
Sparse Core Ops, SparseCore 0:
  115.9 27.0 all-gather.3
  316.9 27.5 all-gather.5
  494.1 127.4 all-reduce.11
where the time goes:
time: 635 us; the launch traced here: 630 us
  waiting for transfers between devices  163 us (26%)
  starting transfers between devices  152 us (24%)
  local copies, waits for them, and re-layouts  132 us (21%)
  other arithmetic  64 us (10%)
  matrix products  61.7 us (10%)
  blocking collectives  40.6 us (6%)
  between operations  15.3 us (2%)
    ppermute x24, starting transfers between devices, padded_2(): before = lax.ppermute(last, axis, up)  111 us
    psum x1, waiting for transfers between devices, shards(): grad_sum, bias_sum = lax.psum((local_grad, local_bias), ('depth', 'rows'))  84.8 us
    slice x71, local copies, waits for them, and re-layouts, taps_product(): padded[row_tap:row_tap + row_count, col_tap:col_tap + col_count]  75 us
    dot_general x207, matrix products, taps_product(): jnp.dot(window, kernel[row_tap, col_tap], preferred_element_type=jnp.floa...  57.3 us
    psum x1, blocking collectives, shards(): grad_sum, bias_sum = lax.psum((local_grad, local_bias), ('depth', 'rows'))  40.6 us
    ppermute x24, starting transfers between devices, padded_2(): after = lax.ppermute(leading, axis, down)  31.6 us
    all_gather x1, waiting for transfers between devices, shards(): res_panels = lax.all_gather(coarse_res[None], 'depth', axis=0, tiled=True)  27.7 us
    ppermute x24, waiting for transfers between devices, padded_2(): before = lax.ppermute(last, axis, up)  25 us
  transfers between devices with their start and end apart: 55, of which 25 were waited for; matrix products, arithmetic and copies ran while one was open for 17% of the time, Pallas kernels for 0%

commit v1 on v0

v1 whole, which is shorter than its diff:
```python
import functools

import jax
import jax.numpy as jnp
from jax import lax
from jax.experimental import pallas as pl
from jax.experimental.pallas import tpu as pltpu
from jax.sharding import PartitionSpec as P

STEP_SIZE = 0.2
MESH = pl.DeviceIdType.MESH
F32, BF16 = jnp.float32, jnp.bfloat16
SRC, ODD, PREV, AHEAD, RELAXED, FIXED = range(6)


def cycle(
    K, Z, cells, init_hbm, fg_hbm, ag_hbm, cot_hbm, kernel_ref, bias_ref,
    states_hbm, adjoints_hbm, gk_ref, gb_ref,
    g, src, init, gprev, y, ynext, cot,
    work, work2, colbuf, derive0, derive1, states, adjoints,
    sf, su, fh, fh_send, fh_recv,
    sc, ch, ch_send, ch_recv,
    vall, dall, eall, rhs, rhs_send, rhs_recv, res, res_send, res_recv, yc, yc_send, yc_recv,
    wf, wr, ga, go, rb, ar_send, ar_recv, big_send, big_recv, in_sem, out_sem,
):
    R, W, C = g.shape
    Rc, Wc = R // 2, W // 2
    d, z = lax.axis_index("depth"), lax.axis_index("rows")
    last = d == K - 1
    NR = ga.shape[0]

    loads = [
        (fg_hbm.at[1], g), (init_hbm, init), (ag_hbm.at[0], y), (cot_hbm, cot),
    ]
    loads = [pltpu.make_async_copy(a, b, in_sem.at[i]) for i, (a, b) in enumerate(loads)]

    def src_load(a):
        return pltpu.make_async_copy(a, src, in_sem.at[4])

    def prev_load():
        return pltpu.make_async_copy(init_hbm, gprev, in_sem.at[5])

    def next_load():
        return pltpu.make_async_copy(cot_hbm, ynext, in_sem.at[6])

    @pl.when(last)
    def _():
        src_load(init_hbm).start()
        next_load().start()

    @pl.when(d < K - 1)
    def _():
        src_load(fg_hbm.at[1]).start()

    for load in (loads[1], loads[0], loads[2], loads[3]):
        load.start()

    @pl.when(d == 0)
    def _():
        prev_load().start()

    barrier = pltpu.get_barrier_semaphore()
    for o in range(1, K):
        pl.semaphore_signal(barrier, inc=1, device_id=(lax.rem(d + o, K), z), device_id_type=MESH)
    for o in range(1, Z):
        pl.semaphore_signal(barrier, inc=1, device_id=(d, lax.rem(z + o, Z)), device_id_type=MESH)

    @pl.when(z == 0)
    def _():
        fh[:, 0] = jnp.zeros_like(fh[:, 0])
        ch[:, 0] = jnp.zeros_like(ch[:, 0])

    @pl.when(z == Z - 1)
    def _():
        fh[:, 1] = jnp.zeros_like(fh[:, 1])
        ch[:, 1] = jnp.zeros_like(ch[:, 1])

    for a in range(3):
        for b in range(3):
            wf[a * C : (a + 1) * C, b * C : (b + 1) * C] = kernel_ref[a, b]
            wr[a * C : (a + 1) * C, b * C : (b + 1) * C] = (
                kernel_ref[2 - a, 2 - b].astype(F32).T.astype(BF16)
            )
    bias = bias_ref[...]

    def remote(a, b, send, recv, target):
        return pltpu.make_async_remote_copy(
            src_ref=a, dst_ref=b, send_sem=send, recv_sem=recv, device_id=target, device_id_type=MESH
        )

    def halo_copies(buf, halo, send, recv, e):
        rows = buf.shape[1]
        up = remote(buf.at[e, 0], halo.at[e, 1], send.at[e, 0], recv.at[e, 1], (d, z - 1))
        down = remote(buf.at[e, rows - 1], halo.at[e, 0], send.at[e, 1], recv.at[e, 0], (d, z + 1))
        return up, down

    def from_up(buf, halo, send, recv, e):
        return remote(buf.at[e, 0], halo.at[e, 0], send.at[e, 1], recv.at[e, 0], (d, z - 1))

    def from_down(buf, halo, send, recv, e):
        return remote(buf.at[e, 0], halo.at[e, 1], send.at[e, 0], recv.at[e, 1], (d, z + 1))

    fine = (sf, fh, fh_send, fh_recv)
    coarse = (sc, ch, ch_send, ch_recv)

    def send_halo(group, e):
        up, down = halo_copies(*group, e)

        @pl.when(z > 0)
        def _():
            up.start()

        @pl.when(z < Z - 1)
        def _():
            down.start()

    def wait_halo(group, e):
        @pl.when(z > 0)
        def _():
            from_up(*group, e).wait_recv()

        @pl.when(z < Z - 1)
        def _():
            from_down(*group, e).wait_recv()

    def wait_sent(group, e):
        up, down = halo_copies(*group, e)

        @pl.when(z > 0)
        def _():
            up.wait_send()

        @pl.when(z < Z - 1)
        def _():
            down.wait_send()

    def col_sum(product, width):
        count = product.shape[0]
        col = lax.broadcasted_iota(jnp.int32, (count, C), 0) % width
        left = jnp.where(col == 0, 0.0, pltpu.roll(product[:, :C], 1, 0))
        right = jnp.where(col == width - 1, 0.0, pltpu.roll(product[:, 2 * C :], count - 1, 0))
        return product[:, C : 2 * C] + left + right

    def conv_own(s, weights):
        rows, width, _ = s.shape
        zero = jnp.zeros((1, width, C), BF16)
        above = jnp.concatenate([zero, s[:-1]], axis=0)
        below = jnp.concatenate([s[1:], zero], axis=0)
        lhs = jnp.concatenate([above, s, below], axis=2).reshape(rows * width, 3 * C)
        product = jnp.dot(lhs, weights[...], preferred_element_type=F32)
        return col_sum(product, width).reshape(rows, width, C)

    def conv_halo(halo, e, weights):
        up = jnp.dot(halo[e, 0], weights[:C], preferred_element_type=F32)
        down = jnp.dot(halo[e, 1], weights[2 * C :], preferred_element_type=F32)
        width = up.shape[0]
        return col_sum(up, width)[None], col_sum(down, width)[None]

    def add_edges(own, up, down):
        inner = [own[1:-1]] if own.shape[0] > 2 else []
        return jnp.concatenate([own[:1] + up] + inner + [own[-1:] + down], axis=0)

    def conv(group, e, weights):
        own = conv_own(group[0][e], weights)
        wait_halo(group, e)
        return add_edges(own, *conv_halo(group[1], e, weights))

    def restrict(ref):
        def part(i, o):
            return ref[i, pl.ds(o, Wc, stride=2), :]

        rows = [
            (part(2 * i, 0) + part(2 * i, 1) + part(2 * i + 1, 0) + part(2 * i + 1, 1)) * 0.25
            for i in range(Rc)
        ]
        return jnp.stack(rows)

    def prolong(value):
        for i in range(Rc):
            colbuf[i, pl.ds(0, Wc, stride=2), :] = value[i]
            colbuf[i, pl.ds(1, Wc, stride=2), :] = value[i]
        wide = colbuf[...]
        return jnp.broadcast_to(wide[:, None], (Rc, 2, W, C)).reshape(R, W, C)

    def spread(buf, send, recv, slot):
        for o in range(1, K):
            remote(buf.at[slot], buf.at[slot], send.at[o], recv.at[slot], (lax.rem(d + o, K), z)).start()

    def wait_panel(buf, send, recv, slot):
        remote(buf.at[slot], buf.at[slot], send.at[0], recv.at[slot], (lax.rem(d + 1, K), z)).wait_recv()

    def wait_spread(buf, send, recv, slot):
        for o in range(1, K):
            remote(
                buf.at[slot], buf.at[slot], send.at[o], recv.at[slot], (lax.rem(d + o, K), z)
            ).wait_send()

    src_load(init_hbm).wait()
    s = jnp.tanh(src[...]).astype(BF16)
    sf[SRC] = s
    src_c = restrict(src)
    sc[K] = jnp.tanh(src_c).astype(BF16)
    pl.semaphore_wait(barrier, K + Z - 2)
    send_halo(fine, SRC)
    send_halo(coarse, K)
    loads[1].wait()
    vall[0] = restrict(init)

    work[...] = src[...] + STEP_SIZE * (conv(fine, SRC, wf) + bias)
    sf[ODD] = jnp.tanh(work[...]).astype(BF16)
    send_halo(fine, ODD)
    tau = src_c + 2.0 * STEP_SIZE * (conv(coarse, K, wf) + bias)
    work[...] = work[...] + STEP_SIZE * (conv(fine, ODD, wf) + bias)
    own_panel = lax.rem(d + 1, K)
    rhs[own_panel] = (restrict(work) - tau).astype(BF16)
    spread(rhs, rhs_send, rhs_recv, own_panel)

    for load in (loads[0], loads[2], loads[3]):
        load.wait()
    to_next = remote(g, gprev, big_send.at[0], big_recv.at[0], (d + 1, z))
    to_prev = remote(y, ynext, big_send.at[1], big_recv.at[1], (d - 1, z))

    @pl.when(d < K - 1)
    def _():
        to_next.start()

    @pl.when(d > 0)
    def _():
        to_prev.start()

    yc[d] = restrict(y)
    yc[K] = restrict(cot)
    spread(yc, yc_send, yc_recv, d)

    def forward(k, carry):
        current = vall[k]
        t = jnp.tanh(current)
        sc[k] = t.astype(BF16)
        send_halo(coarse, k)
        dall[k] = 1.0 - t * t
        summed = conv(coarse, k, wf)

        @pl.when(k != own_panel)
        def _():
            wait_panel(rhs, rhs_send, rhs_recv, k)

        vall[k + 1] = current + 2.0 * STEP_SIZE * (summed + bias) + rhs[k].astype(F32)
        return carry

    lax.fori_loop(0, K, forward, 0)

    @pl.when(d > 0)
    def _():
        remote(g, gprev, big_send.at[0], big_recv.at[0], (d - 1, z)).wait_recv()

    @pl.when(d == 0)
    def _():
        prev_load().wait()

    work[...] = gprev[...] + prolong(vall[d] - restrict(gprev))
    t = jnp.tanh(work[...])
    sf[PREV] = t.astype(BF16)
    send_halo(fine, PREV)
    derive0[...] = 1.0 - t * t

    @pl.when(d < K - 1)
    def _():
        remote(y, ynext, big_send.at[1], big_recv.at[1], (d + 1, z)).wait_recv()

    @pl.when(last)
    def _():
        next_load().wait()

    sf[AHEAD] = ynext[...].astype(BF16)
    send_halo(fine, AHEAD)
    states[0] = work[...] + STEP_SIZE * (conv(fine, PREV, wf) + bias)
    t = jnp.tanh(states[0])
    su[...] = t.astype(BF16)
    derive1[...] = 1.0 - t * t
    work[...] = derive1[...] * conv(fine, AHEAD, wr)
    sf[RELAXED] = (ynext[...] + STEP_SIZE * work[...]).astype(BF16)
    send_halo(fine, RELAXED)
    states[1] = g[...] + prolong(vall[d + 1] - restrict(g))
    states_out = pltpu.make_async_copy(states, states_hbm, out_sem.at[0])
    states_out.start()
    work2[...] = work[...] + derive0[...] * conv(fine, RELAXED, wr)
    res[d] = (STEP_SIZE * restrict(work2)).astype(BF16)
    spread(res, res_send, res_recv, d)

    def panel(k):
        @pl.when(k != d)
        def _():
            wait_panel(res, res_send, res_recv, k)
            wait_panel(yc, yc_send, yc_recv, k)

        return res[k].astype(F32) + (yc[k + 1] - yc[k])

    eall[K] = jnp.zeros_like(eall[K])
    eall[K - 1] = panel(K - 1)

    def backward(i, carry):
        k = K - 2 - i
        error = eall[k + 1]
        slot = K + 1 + i
        sc[slot] = error.astype(BF16)
        send_halo(coarse, slot)
        summed = conv(coarse, slot, wr)
        eall[k] = error + 2.0 * STEP_SIZE * dall[k] * summed + panel(k)
        return carry

    lax.fori_loop(0, K - 1, backward, 0)

    work[...] = ynext[...] + prolong(eall[d + 1])
    sf[FIXED] = work[...].astype(BF16)
    send_halo(fine, FIXED)
    adjoints[0] = y[...] + prolong(eall[d])
    adjoints[1] = work[...] + STEP_SIZE * derive1[...] * conv(fine, FIXED, wr)
    adjoints_out = pltpu.make_async_copy(adjoints, adjoints_hbm, out_sem.at[1])
    adjoints_out.start()

    def col_taps(value):
        rows, width, _ = value.shape
        count = rows * width
        flat = value.astype(F32).reshape(count, C)
        col = lax.broadcasted_iota(jnp.int32, (count, C), 0) % width
        first = jnp.where(col == width - 1, 0.0, pltpu.roll(flat, count - 1, 0))
        third = jnp.where(col == 0, 0.0, pltpu.roll(flat, 1, 0))
        taps = jnp.concatenate([first.astype(BF16), flat.astype(BF16), third.astype(BF16)], axis=1)
        return taps.reshape(rows, width, 3 * C)

    def over_cells(a, b):
        return lax.dot_general(
            a.reshape(R * W, -1), b.reshape(R * W, -1), (((0,), (0,)), ((), ())), preferred_element_type=F32
        )

    taps = col_taps(jnp.concatenate([fh[FIXED, 0][None], sf[FIXED], fh[FIXED, 1][None]], axis=0))
    own = su[...]
    odd = [over_cells(own, taps[2 - a : 2 - a + R]) for a in range(3)]
    around = jnp.concatenate([fh[PREV, 0][None], sf[PREV], fh[PREV, 1][None]], axis=0)
    taps = col_taps(adjoints[1].astype(BF16))
    for a in range(3):
        even = over_cells(around[a : a + R], taps)
        for b in range(3):
            at = (3 * a + b) * C
            cols = slice(b * C, (b + 1) * C)
            ga[at : at + C] = even[:, cols] + odd[a][:, cols]
    total = jnp.sum((adjoints[1] + work[...]).reshape(R * W, C), axis=0, keepdims=True)
    ga[9 * C :] = jnp.zeros((NR - 9 * C, C), F32)
    ga[9 * C : 9 * C + 8] = jnp.broadcast_to(total, (8, C))

    core = lax.rem(d, 2)

    def split(index, stride):
        bit = lax.rem(index // stride, 2)
        return bit, index + (1 - 2 * bit) * stride

    depth_bits = [1 << i for i in range(K.bit_length() - 1)]
    swapped = depth_bits[:1] + depth_bits[1:][::-1]
    plan = []
    for one, two in zip(depth_bits, swapped):
        bit1, to1 = split(d, one)
        bit2, to2 = split(d, two)
        plan.append((bit1 * (1 - core) + bit2 * core, (to1 * (1 - core) + to2 * core, z)))
    for stride in [1 << i for i in range(Z.bit_length() - 1)]:
        bit, to = split(z, stride)
        plan.append((bit, (d, to)))
    n = len(plan)
    offset, length, place = 0, NR, 0
    sends, trail = [], []
    for i, (bit, to) in enumerate(plan):
        half = length // 2
        away = pl.multiple_of(offset + (1 - bit) * half, 8)
        offset = pl.multiple_of(offset + bit * half, 8)
        move = remote(
            ga.at[pl.ds(away, half)], rb.at[pl.ds(place, half)], ar_send.at[i], ar_recv.at[i], to
        )
        move.start()
        move.wait_recv()
        sends.append(move)
        ga[pl.ds(offset, half)] += rb[pl.ds(place, half)]
        trail.append((offset, half, to, away))
        place += half
        length = half
    go[pl.ds(offset, length)] = ga[pl.ds(offset, length)] * (STEP_SIZE / cells)
    for i, (offset, half, to, away) in reversed(list(enumerate(trail))):
        mine, other = go.at[pl.ds(offset, half)], go.at[pl.ds(away, half)]
        move = remote(mine, mine, ar_send.at[n + i], ar_recv.at[n + i], to)
        move.start()
        remote(mine, other, ar_send.at[n + i], ar_recv.at[n + i], to).wait_recv()
        sends.append(move)
    gk_ref[...] = go[: 9 * C]
    gb_ref[...] = go[9 * C : 9 * C + 8]

    for move in sends:
        move.wait_send()
    for e in range(6):
        wait_sent(fine, e)

    def sent(e, carry):
        wait_sent(coarse, e)
        return carry

    lax.fori_loop(0, 2 * K, sent, 0)
    wait_spread(rhs, rhs_send, rhs_recv, own_panel)
    wait_spread(res, res_send, res_recv, d)
    wait_spread(yc, yc_send, yc_recv, d)

    @pl.when(d < K - 1)
    def _():
        to_next.wait_send()

    @pl.when(d > 0)
    def _():
        to_prev.wait_send()

    states_out.wait()
    adjoints_out.wait()


def shards(K, Z, initial, forward_guess, adjoint_guess, cotangent, kernel, conv_bias):
    R, W, C = initial.shape
    Rc, Wc = R // 2, W // 2
    unit = 8 * K * Z
    NR = -(-(9 * C + 8) // unit) * unit
    bits = (K.bit_length() - 1) + (Z.bit_length() - 1)
    vmem, dma = pltpu.VMEM, pltpu.SemaphoreType.DMA
    field, coarse = vmem((R, W, C), F32), (Rc, Wc, C)
    scratch = (
        [field] * 7
        + [field, field, vmem((Rc, W, C), F32), field, field]
        + [vmem((2, R, W, C), F32)] * 2
        + [vmem((6, R, W, C), BF16), vmem((R, W, C), BF16), vmem((6, 2, W, C), BF16)]
        + [dma((6, 2)), dma((6, 2))]
        + [vmem((2 * K,) + coarse, BF16), vmem((2 * K, 2, Wc, C), BF16)]
        + [dma((2 * K, 2)), dma((2 * K, 2))]
        + [vmem((K + 1,) + coarse, F32), vmem((K,) + coarse, F32), vmem((K + 1,) + coarse, F32)]
        + [vmem((K,) + coarse, BF16), dma((K,)), dma((K,))] * 2
        + [vmem((K + 1,) + coarse, F32), dma((K,)), dma((K,))]
        + [vmem((3 * C, 3 * C), BF16)] * 2
        + [vmem((NR, C), F32)] * 3
        + [dma((2 * bits,)), dma((2 * bits,)), dma((2,)), dma((2,)), dma((7,)), dma((2,))]
    )
    any_spec, vmem_spec = pl.BlockSpec(memory_space=pl.ANY), pl.BlockSpec(memory_space=pltpu.VMEM)
    flops = 2 * 9 * C * C * R * W * 12
    states, adjoints, grad, bias = pl.pallas_call(
        functools.partial(cycle, K, Z, R * Z * W),
        out_shape=(
            jax.ShapeDtypeStruct((2, R, W, C), F32),
            jax.ShapeDtypeStruct((2, R, W, C), F32),
            jax.ShapeDtypeStruct((9 * C, C), F32),
            jax.ShapeDtypeStruct((8, C), F32),
        ),
        in_specs=[any_spec] * 4 + [vmem_spec] * 2,
        out_specs=(any_spec, any_spec, vmem_spec, vmem_spec),
        scratch_shapes=scratch,
        compiler_params=pltpu.CompilerParams(
            collective_id=0, has_side_effects=True, vmem_limit_bytes=56 * 1024 * 1024
        ),
        cost_estimate=pl.CostEstimate(flops=flops, bytes_accessed=24 * R * W * C, transcendentals=8 * R * W * C),
    )(initial, forward_guess, adjoint_guess, cotangent, kernel, conv_bias[None])
    return states, adjoints, grad.reshape(3, 3, C, C), bias[0]


def solution(mesh):
    placed = (
        P("rows", None, None),
        P("depth", "rows", None, None),
        P("depth", "rows", None, None),
        P("rows", None, None),
        P(),
        P(),
    )
    return jax.shard_map(
        functools.partial(shards, mesh.shape["depth"], mesh.shape["rows"]),
        mesh=mesh,
        in_specs=placed,
        out_specs=(P("depth", "rows", None, None), P("depth", "rows", None, None), P(), P()),
        check_vma=False,
    )
```

time: 635 us -> 117 us (0.18)
  waiting for transfers between devices: 163 us -> 0 us
  starting transfers between devices: 152 us -> 0 us
  local copies, waits for them, and re-layouts: 132 us -> 5.8 us
  Pallas kernels: 0 us -> 111 us
  other arithmetic: 64 us -> 0 us
  matrix products: 61.7 us -> 0 us
  blocking collectives: 40.6 us -> 0 us
  between operations: 15.3 us -> 0.64 us
    ppermute x52 -> x0, starting transfers between devices: 151 us -> none  [the longest x24 111 us: padded_2(): before = lax.ppermute(last, axis, up)]
    pallas_call x0 -> x1, Pallas kernels: none -> 111 us  [shards(): pl.pallas_call(functools.partial(cycle, K, Z, R * Z * W), out_shape=(jax....]
    psum x1 -> x0, waiting for transfers between devices: 84.8 us -> none  [shards(): grad_sum, bias_sum = lax.psum((local_grad, local_bias), ('depth', 'rows'))]
    slice x98 -> x0, local copies, waits for them, and re-layouts: 80 us -> none  [the longest x71 75 us: taps_product(): padded[row_tap:row_tap + row_count, col_tap:col_tap + col_count]]
    dot_general x225 -> x0, matrix products: 61.7 us -> none  [the longest x207 57.3 us: taps_product(): jnp.dot(window, kernel[row_tap, col_tap], preferred_element_type=jnp.floa...]
    ppermute x52 -> x0, waiting for transfers between devices: 41.6 us -> none  [the longest x24 25 us: padded_2(): before = lax.ppermute(last, axis, up)]
    psum x1 -> x0, blocking collectives: 40.6 us -> none  [shards(): grad_sum, bias_sum = lax.psum((local_grad, local_bias), ('depth', 'rows'))]
    all_gather x2 -> x0, waiting for transfers between devices: 36.9 us -> none  [the longest x1 27.7 us: shards(): res_panels = lax.all_gather(coarse_res[None], 'depth', axis=0, tiled=True)]
  transfers between devices with their start and end apart: 55 -> 0, of which waited for: 25 -> 0; matrix products, arithmetic and copies ran while one was open for 17% -> 0% of each run, Pallas kernels for 0% -> 0%
where the time goes in v1:
time: 117 us
  Pallas kernels  111 us (95%)
  local copies, waits for them, and re-layouts  5.8 us (5%)
    pallas_call x1, Pallas kernels, shards(): pl.pallas_call(functools.partial(cycle, K, Z, R * Z * W), out_shape=(jax....  111 us
    unnamed x7, local copies, waits for them, and re-layouts  4.62 us

profile of v1, /device:TPU:0, one launch (start us, length us, event | category | flops | bytes accessed | tf_op | source)
XLA Modules:
  0.0 117.0 jit_solution(880809019280301671)
XLA Ops:
  0.6 110.5 %shard_map.93 = (f32[2,4,256,128]{3,2,1,0:T(8,128)}, f32[2,4,256,128]{3,2,1,0:T(8,128)}, f32[1152,128]{1,0:T(8,128)}, f32[8,128]{1,0:T(8,128)}) custom-call(f32[4,256,128]{2,1,0:T(8,128)} %init_hbm.1, f32[2,4,256,128]{3,2,1,0:T(8,128)} %fg_hbm.1, f32[2,4,256,128]{3,2,1,0:T(8,128)} %ag_hbm.1, f32[4,256,128]{2,1,0:T(8,128)} %cot_hbm.1, ...), custom_call_target="tpu_custom_call" | custom-call | flops 3623878656 | bytes 3145728 | tf_op jit(solution)/shard_map/pallas_call | solution.py:445
  111.2 1.2 %slice_bitcast_fusion = f32[128]{0:T(128)} fusion(f32[8,128]{1,0:T(8,128)} %get-tuple-element.11), kind=kLoop, calls=%fused_computation | loop fusion | bytes 1024 | tf_op jit(solution)/shard_map/squeeze | solution.py:461
  112.3 0.0 copy-start
  112.3 2.4 %copy.13 = f32[2,4,256,128]{3,2,1,0:T(8,128)} copy(f32[2,4,256,128]{3,2,1,0:T(8,128)} %get-tuple-element.16) | data formatting | bytes 2097152
  114.7 0.0 copy-done
  114.7 0.0 copy-start.1
  114.7 1.0 copy.14
  115.7 0.5 copy-done.1
  116.2 0.8 copy.15
Async XLA Ops:
  112.3 2.4 %copy-start = (f32[2,4,256,128]{3,2,1,0:T(8,128)S(1)}, f32[2,4,256,128]{3,2,1,0:T(8,128)}, u32[]{:S(2)}) copy-start(f32[2,4,256,128]{3,2,1,0:T(8,128)} %get-tuple-element.17) | copy-start | bytes 3145732
  114.7 1.4 %copy-start.1 = (f32[1152,128]{1,0:T(8,128)S(1)}, f32[1152,128]{1,0:T(8,128)}, u32[]{:S(2)}) copy-start(f32[1152,128]{1,0:T(8,128)} %get-tuple-element.10) | copy-start | bytes 1769476

commit v2 on v1

v2 whole, which is shorter than its diff:
```python
import functools

import jax
import jax.numpy as jnp
from jax import lax
from jax.experimental import pallas as pl
from jax.experimental.pallas import tpu as pltpu
from jax.sharding import PartitionSpec as P

STEP_SIZE = 0.2
MESH = pl.DeviceIdType.MESH
F32, BF16 = jnp.float32, jnp.bfloat16
SRC, ODD, PREV, AHEAD, RELAXED, FIXED = range(6)


def cycle(
    K, Z, cells, init_hbm, fg_hbm, ag_hbm, cot_hbm, kernel_ref, bias_ref,
    states_hbm, adjoints_hbm, gk_ref,
    g, src, init, gprev, y, ynext, cot,
    work, work2, colbuf, derive0, derive1, states, adjoints,
    sf, su, fh, fh_send, fh_recv,
    st, th, th_send, th_recv,
    sc, ch, ch_send, ch_recv,
    vall, dall, fall, rprev, rnext, rown,
    rhs_all, rhs, rhs_send, rhs_recv, res_all, res, res_send, res_recv, yc_all, yc, yc_send, yc_recv,
    vx, vx_send, vx_recv, fx, fx_send, fx_recv,
    wf, wr, prev_t, odd_t, ga, rb1, rb2, rb3, gob, ar_send, ar_recv, big_send, big_recv, in_sem, out_sem,
):
    R, W, C = g.shape
    Rc, Wc = R // 2, W // 2
    Rh = Rc // 2
    d, z = lax.axis_index("depth"), lax.axis_index("rows")
    last = d == K - 1
    NR = ga.shape[0]
    core = lax.rem(d, 2)
    peer = d + 1 - 2 * core
    pair = d - core
    mine = pl.ds(core * Rh, Rh)

    loads = [
        (fg_hbm.at[1], g), (init_hbm, init), (ag_hbm.at[0], y), (cot_hbm, cot),
    ]
    loads = [pltpu.make_async_copy(a, b, in_sem.at[i]) for i, (a, b) in enumerate(loads)]

    def src_load(a):
        return pltpu.make_async_copy(a, src, in_sem.at[4])

    def prev_load():
        return pltpu.make_async_copy(init_hbm, gprev, in_sem.at[5])

    def next_load():
        return pltpu.make_async_copy(cot_hbm, ynext, in_sem.at[6])

    @pl.when(last)
    def _():
        src_load(init_hbm).start()
        next_load().start()

    @pl.when(d < K - 1)
    def _():
        src_load(fg_hbm.at[1]).start()

    for load in loads:
        load.start()

    @pl.when(d == 0)
    def _():
        prev_load().start()

    has_up, has_down = core + z > 0, z + core < Z
    up_target, down_target = (peer, z - 1 + core), (peer, z + core)

    barrier = pltpu.get_barrier_semaphore()
    for o in range(1, K):
        pl.semaphore_signal(barrier, inc=1, device_id=(lax.rem(d + o, K), z), device_id_type=MESH)
    for o in range(1, Z):
        pl.semaphore_signal(barrier, inc=1, device_id=(d, lax.rem(z + o, Z)), device_id_type=MESH)
    across = z + 2 * core - 1
    has_across = (across >= 0) & (across < Z)

    @pl.when(has_across)
    def _():
        pl.semaphore_signal(barrier, inc=1, device_id=(peer, across), device_id_type=MESH)

    @pl.when(z == 0)
    def _():
        fh[:, 0] = jnp.zeros_like(fh[:, 0])
        th[:, 0] = jnp.zeros_like(th[:, 0])

    @pl.when(z == Z - 1)
    def _():
        fh[:, 1] = jnp.zeros_like(fh[:, 1])
        th[:, 1] = jnp.zeros_like(th[:, 1])

    @pl.when(core + z == 0)
    def _():
        ch[:, 0] = jnp.zeros_like(ch[:, 0])

    @pl.when(z + core == Z)
    def _():
        ch[:, 1] = jnp.zeros_like(ch[:, 1])

    for a in range(3):
        for b in range(3):
            wf[a * C : (a + 1) * C, b * C : (b + 1) * C] = kernel_ref[a, b]
    bias = bias_ref[...]

    def remote(a, b, send, recv, target):
        return pltpu.make_async_remote_copy(
            src_ref=a, dst_ref=b, send_sem=send, recv_sem=recv, device_id=target, device_id_type=MESH
        )

    rows_line = (z > 0, z < Z - 1, (d, z - 1), (d, z + 1))
    fine = (sf, fh, fh_send, fh_recv) + rows_line
    tau_group = (st, th, th_send, th_recv) + rows_line
    coarse = (sc, ch, ch_send, ch_recv, has_up, has_down, up_target, down_target)

    def halo_copies(group, e):
        buf, halo, send, recv, _, _, above, below = group
        rows = buf.shape[1]
        up = remote(buf.at[e, 0], halo.at[e, 1], send.at[e, 0], recv.at[e, 1], above)
        down = remote(buf.at[e, rows - 1], halo.at[e, 0], send.at[e, 1], recv.at[e, 0], below)
        return up, down

    def send_halo(group, e):
        up, down = halo_copies(group, e)

        @pl.when(group[4])
        def _():
            up.start()

        @pl.when(group[5])
        def _():
            down.start()

    def wait_halo(group, e):
        buf, halo, send, recv, from_up, from_down, above, below = group

        @pl.when(from_up)
        def _():
            remote(buf.at[e, 0], halo.at[e, 0], send.at[e, 1], recv.at[e, 0], above).wait_recv()

        @pl.when(from_down)
        def _():
            remote(buf.at[e, 0], halo.at[e, 1], send.at[e, 0], recv.at[e, 1], below).wait_recv()

    def wait_sent(group, e):
        up, down = halo_copies(group, e)

        @pl.when(group[4])
        def _():
            up.wait_send()

        @pl.when(group[5])
        def _():
            down.wait_send()

    def col_sum(product, width):
        count = product.shape[0]
        col = lax.broadcasted_iota(jnp.int32, (count, C), 0) % width
        left = jnp.where(col == 0, 0.0, pltpu.roll(product[:, :C], 1, 0))
        right = jnp.where(col == width - 1, 0.0, pltpu.roll(product[:, 2 * C :], count - 1, 0))
        return product[:, C : 2 * C] + left + right

    def conv_own(s, weights):
        rows, width, _ = s.shape
        zero = jnp.zeros((1, width, C), BF16)
        above = jnp.concatenate([zero, s[:-1]], axis=0)
        below = jnp.concatenate([s[1:], zero], axis=0)
        lhs = jnp.concatenate([above, s, below], axis=2).reshape(rows * width, 3 * C)
        product = jnp.dot(lhs, weights[...], preferred_element_type=F32)
        return col_sum(product, width).reshape(rows, width, C)

    def conv_halo(halo, e, weights):
        up = jnp.dot(halo[e, 0], weights[:C], preferred_element_type=F32)
        down = jnp.dot(halo[e, 1], weights[2 * C :], preferred_element_type=F32)
        width = up.shape[0]
        return col_sum(up, width)[None], col_sum(down, width)[None]

    def add_edges(own, up, down):
        if own.shape[0] == 1:
            return own + up + down
        inner = [own[1:-1]] if own.shape[0] > 2 else []
        return jnp.concatenate([own[:1] + up] + inner + [own[-1:] + down], axis=0)

    def conv(group, e, weights, fill=None):
        buf, halo = group[:2]
        if buf.shape[1] == 1:
            own = jnp.dot(buf[e, 0], weights[C : 2 * C], preferred_element_type=F32)
            if fill is not None:
                fill()
            wait_halo(group, e)
            sides = jnp.concatenate([halo[e, 0], halo[e, 1]], axis=1)
            outer = jnp.concatenate([weights[:C], weights[2 * C :]], axis=0)
            product = own + jnp.dot(sides, outer, preferred_element_type=F32)
            return col_sum(product, product.shape[0])[None]
        own = conv_own(buf[e], weights)
        if fill is not None:
            fill()
        wait_halo(group, e)
        return add_edges(own, *conv_halo(halo, e, weights))

    def restrict(ref):
        def part(i, o):
            return ref[i, pl.ds(o, Wc, stride=2), :]

        rows = [
            (part(2 * i, 0) + part(2 * i, 1) + part(2 * i + 1, 0) + part(2 * i + 1, 1)) * 0.25
            for i in range(Rc)
        ]
        return jnp.stack(rows)

    def prolong(value):
        for i in range(Rc):
            colbuf[i, pl.ds(0, Wc, stride=2), :] = value[i]
            colbuf[i, pl.ds(1, Wc, stride=2), :] = value[i]
        wide = colbuf[...]
        return jnp.broadcast_to(wide[:, None], (Rc, 2, W, C)).reshape(R, W, C)

    def panel_copies(full, buf, send, recv, slot):
        copies = []
        for o in range(1, K):
            to = lax.rem(d + o, K)
            part = full.at[pl.ds(lax.rem(to, 2) * Rh, Rh)]
            copies.append(remote(part, buf.at[slot], send.at[o], recv.at[slot], (to, z)))
        return copies

    def spread(full, buf, send, recv, slot):
        for copy in panel_copies(full, buf, send, recv, slot):
            copy.start()
        buf[slot] = full[mine]

    def wait_spread(full, buf, send, recv, slot):
        for copy in panel_copies(full, buf, send, recv, slot):
            copy.wait_send()

    def wait_panel(buf, send, recv, slot):
        remote(buf.at[slot], buf.at[slot], send.at[0], recv.at[slot], (peer, z)).wait_recv()

    def share_copy(buf, send, recv, j):
        part = buf.at[j, mine]
        return remote(part, part, send.at[j], recv.at[j], (peer, z))

    def share(buf, send, recv, k, value):
        @pl.when((k >= pair) & (k <= pair + 2))
        def _():
            buf[k - pair, mine] = value
            share_copy(buf, send, recv, k - pair).start()

    def wait_shared(buf, send, recv):
        for j in range(3):
            share_copy(buf, send, recv, j).wait_recv()

    @pl.when(last)
    def _():
        src_load(init_hbm).wait()

    @pl.when(d < K - 1)
    def _():
        src_load(fg_hbm.at[1]).wait()

    sf[SRC] = jnp.tanh(src[...]).astype(BF16)
    pl.semaphore_wait(barrier, K + Z - 2 + has_across.astype(jnp.int32))

    send_halo(fine, SRC)
    src_c = restrict(src)
    st[0] = jnp.tanh(src_c).astype(BF16)
    send_halo(tau_group, 0)

    loads[0].wait()
    loads[2].wait()
    to_next = remote(g, gprev, big_send.at[0], big_recv.at[0], (d + 1, z))
    to_prev = remote(y, ynext, big_send.at[1], big_recv.at[1], (d - 1, z))

    @pl.when(d < K - 1)
    def _():
        to_next.start()

    @pl.when(d > 0)
    def _():
        to_prev.start()

    work[...] = src[...] + STEP_SIZE * (conv(fine, SRC, wf) + bias)
    sf[ODD] = jnp.tanh(work[...]).astype(BF16)
    send_halo(fine, ODD)
    tau = src_c + 2.0 * STEP_SIZE * (conv(tau_group, 0, wf) + bias)
    work[...] = work[...] + STEP_SIZE * (conv(fine, ODD, wf) + bias)
    own_panel = lax.rem(d + 1, K)
    rhs_all[...] = (restrict(work) - tau).astype(BF16)
    spread(rhs_all, rhs, rhs_send, rhs_recv, own_panel)

    loads[1].wait()
    colbuf[:, :Wc] = restrict(init)
    vall[0] = colbuf[mine, :Wc]
    share(vx, vx_send, vx_recv, 0, vall[0])
    loads[3].wait()
    rown[...] = restrict(y)
    yc_all[...] = rown[...].astype(BF16)
    spread(yc_all, yc, yc_send, yc_recv, d)
    for a in range(3):
        for b in range(3):
            wr[a * C : (a + 1) * C, b * C : (b + 1) * C] = (
                kernel_ref[2 - a, 2 - b].astype(F32).T.astype(BF16)
            )

    def ahead_arrives():
        @pl.when(d < K - 1)
        def _():
            remote(y, ynext, big_send.at[1], big_recv.at[1], (d + 1, z)).wait_recv()

        @pl.when(last)
        def _():
            next_load().wait()

        sf[AHEAD] = ynext[...].astype(BF16)
        send_halo(fine, AHEAD)

    def ahead_conv():
        work2[...] = conv(fine, AHEAD, wr)

    def prev_arrives():
        @pl.when(d > 0)
        def _():
            remote(g, gprev, big_send.at[0], big_recv.at[0], (d - 1, z)).wait_recv()

        @pl.when(d == 0)
        def _():
            prev_load().wait()

        rprev[...] = restrict(gprev)

    def next_restricted():
        rnext[...] = restrict(ynext)

    def filled(k, steps, tasks):
        for i, task in enumerate(tasks):
            pl.when(k == max(0, steps - len(tasks) + i))(task)

    def forward(k, current):
        t = jnp.tanh(current)
        sc[k] = t.astype(BF16)
        send_halo(coarse, k)
        dall[k] = 1.0 - t * t

        def fill():
            filled(k, K, [ahead_arrives, next_restricted, ahead_conv, prev_arrives])

        summed = conv(coarse, k, wf, fill)

        @pl.when(k != own_panel)
        def _():
            wait_panel(rhs, rhs_send, rhs_recv, k)

        value = current + 2.0 * STEP_SIZE * (summed + bias) + rhs[k].astype(F32)
        share(vx, vx_send, vx_recv, k + 1, value)
        return value

    lax.fori_loop(0, K, forward, vall[0])
    wait_shared(vx, vx_send, vx_recv)

    work[...] = gprev[...] + prolong(vx[core] - rprev[...])
    t = jnp.tanh(work[...])
    sf[PREV] = t.astype(BF16)
    send_halo(fine, PREV)
    derive0[...] = 1.0 - t * t
    states[0] = work[...] + STEP_SIZE * (conv(fine, PREV, wf) + bias)
    t = jnp.tanh(states[0])
    su[...] = t.astype(BF16)
    slope = 1.0 - t * t
    derive1[...] = slope
    work[...] = slope * work2[...]
    sf[RELAXED] = (ynext[...] + STEP_SIZE * work[...]).astype(BF16)
    send_halo(fine, RELAXED)
    work2[...] = work[...] + derive0[...] * conv(fine, RELAXED, wr)
    res_all[...] = (STEP_SIZE * restrict(work2)).astype(BF16)
    spread(res_all, res, res_send, res_recv, d)
    colbuf[:, :Wc] = restrict(cot)
    fall[K] = colbuf[mine, :Wc]
    share(fx, fx_send, fx_recv, K, fall[K])

    def panel(k):
        @pl.when(k != d)
        def _():
            wait_panel(res, res_send, res_recv, k)
            wait_panel(yc, yc_send, yc_recv, k)

        return res[k].astype(F32)

    states_out = pltpu.make_async_copy(states, states_hbm, out_sem.at[0])

    def corrected_state():
        states[1] = g[...] + prolong(vx[core + 1] - restrict(g))
        states_out.start()

    def turn(rows, out):
        for i, row in enumerate(rows):
            out[:, i * W : (i + 1) * W] = row.astype(F32).T.astype(BF16)

    def turn_prev():
        turn([fh[PREV, 0]] + [sf[PREV, i] for i in range(R)] + [fh[PREV, 1]], prev_t)

    def turn_odd():
        turn([su[i] for i in range(R)], odd_t)

    value = fall[K] + panel(K - 1)
    share(fx, fx_send, fx_recv, K - 1, value)

    def backward(i, later):
        k = K - 2 - i
        sc[K + i] = (later - yc[k + 1].astype(F32)).astype(BF16)
        send_halo(coarse, K + i)

        def fill():
            filled(i, K - 1, [corrected_state, turn_prev, turn_odd])

        summed = conv(coarse, K + i, wr, fill)
        value = later + 2.0 * STEP_SIZE * dall[k] * summed + panel(k)
        share(fx, fx_send, fx_recv, k, value)
        return value

    lax.fori_loop(0, K - 1, backward, value)
    wait_shared(fx, fx_send, fx_recv)

    work[...] = ynext[...] + prolong(fx[core + 1] - rnext[...])
    sf[FIXED] = work[...].astype(BF16)
    send_halo(fine, FIXED)
    adjoints[0] = y[...] + prolong(fx[core] - rown[...])
    adjoints[1] = work[...] + STEP_SIZE * derive1[...] * conv(fine, FIXED, wr)
    adjoints_out = pltpu.make_async_copy(adjoints, adjoints_hbm, out_sem.at[1])
    adjoints_out.start()

    def col_taps(value):
        rows, width, _ = value.shape
        count = rows * width
        flat = value.astype(F32).reshape(count, C)
        col = lax.broadcasted_iota(jnp.int32, (count, C), 0) % width
        first = jnp.where(col == width - 1, 0.0, pltpu.roll(flat, count - 1, 0))
        third = jnp.where(col == 0, 0.0, pltpu.roll(flat, 1, 0))
        taps = jnp.concatenate([first.astype(BF16), flat.astype(BF16), third.astype(BF16)], axis=1)
        return taps.reshape(rows, width, 3 * C)

    taps = col_taps(jnp.concatenate([fh[FIXED, 0][None], sf[FIXED], fh[FIXED, 1][None]], axis=0))
    taps = jnp.concatenate([taps[2 - a : 2 - a + R] for a in range(3)], axis=2).reshape(R * W, 9 * C)
    odd = jnp.dot(odd_t[...], taps, preferred_element_type=F32)
    taps = col_taps(adjoints[1].astype(BF16)).reshape(R * W, 3 * C)
    for a in range(3):
        even = jnp.dot(prev_t[:, a * W : (a + R) * W], taps, preferred_element_type=F32)
        for b in range(3):
            at = (3 * a + b) * C
            ga[at : at + C] = even[:, b * C : (b + 1) * C] + odd[:, at : at + C]
    total = jnp.sum((adjoints[1] + work[...]).reshape(R * W, C), axis=0, keepdims=True)
    ga[9 * C :] = jnp.zeros((NR - 9 * C, C), F32)
    ga[9 * C : 9 * C + 8] = jnp.broadcast_to(total, (8, C))

    chips = K // 2
    chip = d // 2
    half, block = NR // 2, NR // K
    unit = block // Z
    sends = []

    def launch(move):
        move.start()
        sends.append(move)

    def at(offset, length):
        return ga.at[pl.ds(pl.multiple_of(offset, 8), length)]

    low = core * half
    move = remote(at((1 - core) * half, half), rb1, ar_send.at[0], ar_recv.at[0], (peer, z))
    launch(move)
    move.wait_recv()
    ga[pl.ds(pl.multiple_of(low, 8), half)] += rb1[...]
    moves = []
    for o in range(1, chips):
        to = lax.rem(chip + o, chips)
        move = remote(
            at(low + to * block, block), rb2.at[o], ar_send.at[o], ar_recv.at[o], (2 * to + core, z)
        )
        launch(move)
        moves.append(move)
    low = low + chip * block
    for move in moves:
        move.wait_recv()
    total = ga[pl.ds(pl.multiple_of(low, 8), block)]
    for o in range(1, chips):
        total = total + rb2[o]
    ga[pl.ds(pl.multiple_of(low, 8), block)] = total
    moves = []
    for o in range(1, Z):
        to = lax.rem(z + o, Z)
        move = remote(
            at(low + to * unit, unit), rb3.at[o], ar_send.at[chips + o], ar_recv.at[chips + o], (d, to)
        )
        launch(move)
        moves.append(move)
    low = low + z * unit
    for move in moves:
        move.wait_recv()
    total = ga[pl.ds(pl.multiple_of(low, 8), unit)]
    for o in range(1, Z):
        total = total + rb3[o]
    spare = gob.shape[1] - unit
    total = total * (STEP_SIZE / cells)
    row = low + lax.broadcasted_iota(jnp.int32, (unit, C), 0)
    total = jnp.where(row == 9 * C + 1, total - total.astype(BF16).astype(F32), total)
    if spare:
        total = jnp.concatenate([total, jnp.zeros((spare, C), F32)], axis=0)
    line = core * chips + chip
    gob[line * Z + z] = total.astype(BF16)

    base = chips + Z
    moves = []
    for o in range(1, Z):
        part = gob.at[line * Z + z]
        launch(remote(part, part, ar_send.at[base + o], ar_recv.at[base + o], (d, lax.rem(z + o, Z))))
        part = gob.at[line * Z + lax.rem(z + Z - o, Z)]
        moves.append(remote(part, part, ar_send.at[base + o], ar_recv.at[base + o], (d, lax.rem(z + o, Z))))
    for move in moves:
        move.wait_recv()
    base = base + Z
    moves = []
    for o in range(1, chips):
        to = (2 * lax.rem(chip + o, chips) + core, z)
        part = gob.at[pl.ds(line * Z, Z)]
        launch(remote(part, part, ar_send.at[base + o], ar_recv.at[base + o], to))
        part = gob.at[pl.ds((core * chips + lax.rem(chip + chips - o, chips)) * Z, Z)]
        moves.append(remote(part, part, ar_send.at[base + o], ar_recv.at[base + o], to))
    for move in moves:
        move.wait_recv()
    part = gob.at[pl.ds(core * chips * Z, chips * Z)]
    launch(remote(part, part, ar_send.at[base], ar_recv.at[base], (peer, z)))
    part = gob.at[pl.ds((1 - core) * chips * Z, chips * Z)]
    remote(part, part, ar_send.at[base], ar_recv.at[base], (peer, z)).wait_recv()
    for i in range(K * Z):
        gk_ref[i * unit : (i + 1) * unit] = gob[i].astype(F32)[:unit]

    for move in sends:
        move.wait_send()
    for e in range(6):
        wait_sent(fine, e)
    wait_sent(tau_group, 0)

    def sent(e, carry):
        wait_sent(coarse, e)
        return carry

    lax.fori_loop(0, 2 * K - 1, sent, 0)
    wait_spread(rhs_all, rhs, rhs_send, rhs_recv, own_panel)
    wait_spread(res_all, res, res_send, res_recv, d)
    wait_spread(yc_all, yc, yc_send, yc_recv, d)
    for j in range(3):
        share_copy(vx, vx_send, vx_recv, j).wait_send()
        share_copy(fx, fx_send, fx_recv, j).wait_send()

    @pl.when(d < K - 1)
    def _():
        to_next.wait_send()

    @pl.when(d > 0)
    def _():
        to_prev.wait_send()

    states_out.wait()
    adjoints_out.wait()


def hand_over(states, adjoints, gradient, states_out, adjoints_out, gk_out, gb_out, sems):
    taps = gk_out.shape[0]
    pairs = [(states.at[0], states_out.at[0]), (states.at[1], states_out.at[1])]
    pairs += [(adjoints.at[0], adjoints_out.at[0]), (adjoints.at[1], adjoints_out.at[1])]
    pairs += [(gradient.at[pl.ds(0, taps)], gk_out)]
    copies = [pltpu.make_async_copy(a, b, sems.at[i]) for i, (a, b) in enumerate(pairs)]
    for copy in copies:
        copy.start()
    last = pltpu.make_async_copy(gradient.at[pl.ds(taps, 8)], gb_out, sems.at[len(pairs)])
    last.start()
    for copy in copies:
        copy.wait()
    last.wait()


def shards(K, Z, initial, forward_guess, adjoint_guess, cotangent, kernel, conv_bias):
    R, W, C = initial.shape
    Rc, Wc = R // 2, W // 2
    Rh = Rc // 2
    unit = -(-(9 * C + 8) // (8 * K * Z)) * 8
    NR = unit * K * Z
    chips = K // 2
    vmem, dma = pltpu.VMEM, pltpu.SemaphoreType.DMA
    field, both = vmem((R, W, C), F32), vmem((Rc, Wc, C), F32)
    panels = [vmem((Rc, Wc, C), BF16), vmem((K, Rh, Wc, C), BF16), dma((K,)), dma((K,))]
    shared = [vmem((3, Rc, Wc, C), F32), dma((3,)), dma((3,))]
    points = 1 + 2 * (chips + Z) + chips
    scratch = (
        [field] * 7
        + [field, field, vmem((Rc, W, C), F32), field, field]
        + [vmem((2, R, W, C), F32)] * 2
        + [vmem((6, R, W, C), BF16), vmem((R, W, C), BF16), vmem((6, 2, W, C), BF16)]
        + [dma((6, 2)), dma((6, 2))]
        + [vmem((1, Rc, Wc, C), BF16), vmem((1, 2, Wc, C), BF16), dma((1, 2)), dma((1, 2))]
        + [vmem((2 * K, Rh, Wc, C), BF16), vmem((2 * K, 2, Wc, C), BF16)]
        + [dma((2 * K, 2)), dma((2 * K, 2))]
        + [vmem((K + 1, Rh, Wc, C), F32), vmem((K, Rh, Wc, C), F32), vmem((K + 1, Rh, Wc, C), F32)]
        + [both] * 3
        + panels * 3
        + shared * 2
        + [vmem((3 * C, 3 * C), BF16)] * 2
        + [vmem((C, (R + 2) * W), BF16), vmem((C, R * W), BF16)]
        + [vmem((NR, C), F32), vmem((NR // 2, C), F32), vmem((chips, NR // K, C), F32), vmem((Z, unit, C), F32)]
        + [vmem((K * Z, -(-unit // 16) * 16, C), BF16)]
        + [dma((points,)), dma((points,)), dma((2,)), dma((2,)), dma((7,)), dma((2,))]
    )
    any_spec, vmem_spec = pl.BlockSpec(memory_space=pl.ANY), pl.BlockSpec(memory_space=pltpu.VMEM)
    flops = 2 * 9 * C * C * R * W * 12
    pair = jax.ShapeDtypeStruct((2, R, W, C), F32)
    states, adjoints, gradient = pl.pallas_call(
        functools.partial(cycle, K, Z, R * Z * W),
        out_shape=(pair, pair, jax.ShapeDtypeStruct((NR, C), F32)),
        in_specs=[any_spec] * 4 + [vmem_spec] * 2,
        out_specs=(any_spec, any_spec, vmem_spec),
        scratch_shapes=scratch,
        compiler_params=pltpu.CompilerParams(
            collective_id=0, has_side_effects=True, vmem_limit_bytes=44 * 1024 * 1024
        ),
        cost_estimate=pl.CostEstimate(flops=flops, bytes_accessed=24 * R * W * C, transcendentals=8 * R * W * C),
    )(initial, forward_guess, adjoint_guess, cotangent, kernel, conv_bias[None])
    states, adjoints, grad, bias = pl.pallas_call(
        hand_over,
        out_shape=(pair, pair, jax.ShapeDtypeStruct((9 * C, C), F32), jax.ShapeDtypeStruct((8, C), F32)),
        in_specs=[any_spec] * 3,
        out_specs=(any_spec,) * 4,
        scratch_shapes=[dma((6,))],
        cost_estimate=pl.CostEstimate(flops=0, bytes_accessed=40 * R * W * C, transcendentals=0),
    )(states, adjoints, gradient)
    return states, adjoints, grad.reshape(3, 3, C, C), bias[0] + bias[1]


def solution(mesh):
    placed = (
        P("rows", None, None),
        P("depth", "rows", None, None),
        P("depth", "rows", None, None),
        P("rows", None, None),
        P(),
        P(),
    )
    return jax.shard_map(
        functools.partial(shards, mesh.shape["depth"], mesh.shape["rows"]),
        mesh=mesh,
        in_specs=placed,
        out_specs=(P("depth", "rows", None, None), P("depth", "rows", None, None), P(), P()),
        check_vma=False,
    )
```

time: 117 us -> 187 us (1.60)
  Pallas kernels: 111 us -> 176 us
  local copies, waits for them, and re-layouts: 5.8 us -> 8.98 us
    pallas_call x1 -> x2, Pallas kernels: 111 us -> 176 us  [the longest x1 93.2 us: shards(): pl.pallas_call(functools.partial(cycle, K, Z, R * Z * W), out_shape=(pair...]
    unnamed x7 -> x18, local copies, waits for them, and re-layouts: 4.62 us -> 8.98 us
where the time goes in v2:
time: 187 us
  Pallas kernels  176 us (94%)
  local copies, waits for them, and re-layouts  8.98 us (5%)
    pallas_call x1, Pallas kernels, shards(): pl.pallas_call(functools.partial(cycle, K, Z, R * Z * W), out_shape=(pair...  93.2 us
    pallas_call x1, Pallas kernels, shards(): pl.pallas_call(hand_over, out_shape=(pair, pair, jax.ShapeDtypeStruct((9...  82.7 us
    unnamed x18, local copies, waits for them, and re-layouts  8.98 us

profile of v2, /device:TPU:0, one launch (start us, length us, event | category | flops | bytes accessed | tf_op | source)
XLA Modules:
  0.0 186.7 jit_solution(6004746832191790639)
XLA Ops:
  0.6 0.0 copy-start.8
  0.6 0.6 copy-done.8
  1.3 0.0 copy-start.3
  1.3 1.2 copy-done.3
  2.5 0.0 copy-start.4
  2.5 1.2 copy-done.4
  3.7 0.0 copy-start.5
  3.7 1.0 copy-done.5
  4.8 0.0 copy-start.6
  4.8 1.0 copy-done.6
  5.8 0.0 copy-start.7
  5.8 1.0 copy-done.7
  6.8 93.2 %shard_map.93 = (f32[2,4,256,128]{3,2,1,0:T(8,128)S(1)}, f32[2,4,256,128]{3,2,1,0:T(8,128)S(1)}, f32[1280,128]{1,0:T(8,128)S(1)}) custom-call(f32[4,256,128]{2,1,0:T(8,128)S(1)} %copy-done.5, f32[2,4,256,128]{3,2,1,0:T(8,128)S(1)} %copy-done.3, f32[2,4,256,128]{3,2,1,0:T(8,128)S(1)} %copy-done.4, f32[4,256,128]{2,1,0:T(8,128)S(1)} %copy-done.6, ...), custom_call_target="tpu_custom_call" | custom-call | flops 3623878656 | bytes 3145728 | tf_op jit(solution)/shard_map/pallas_call | solution.py:616
  100.0 0.0 copy-start
  100.0 1.0 copy-done
  100.9 0.0 copy-start.1
  100.9 1.0 copy-done.1
  102.0 0.0 copy-start.2
  102.0 0.8 copy-done.2
  102.8 82.7 %shard_map.94 = (f32[2,4,256,128]{3,2,1,0:T(8,128)}, f32[2,4,256,128]{3,2,1,0:T(8,128)}, f32[1152,128]{1,0:T(8,128)}, f32[8,128]{1,0:T(8,128)}) custom-call(f32[2,4,256,128]{3,2,1,0:T(8,128)} %copy-done, f32[2,4,256,128]{3,2,1,0:T(8,128)} %copy-done.1, f32[1280,128]{1,0:T(8,128)} %copy-done.2), custom_call_target="tpu_custom_call" | custom-call | bytes 5242880 | tf_op jit(solution)/shard_map/pallas_call | solution.py:627
  185.5 1.3 add_bitcast_fusion
Async XLA Ops:
  0.6 0.7 copy-start.8
  1.3 1.2 copy-start.3
  2.5 1.2 copy-start.4
  3.7 1.0 copy-start.5
  4.8 1.0 copy-start.6
  5.8 1.0 copy-start.7
  100.0 1.0 copy-start
  100.9 1.0 copy-start.1
  102.0 0.9 copy-start.2
